TPU v7x, 32 devices: a whole 2x2x4 slice. The times are simulated.
32 devices in a mesh: dp: 8 (over y, x, core), tensor: 4 (over z).
Axes of the slice: x: 2, y: 2, z: 4, core: 2. Of those that a mesh axis runs over, the one named last changes fastest.
Arguments:
- tokens: bfloat16 [16384, 768], P(('dp', 'tensor')), may hold values from -6 to 6
- segment_ids: int32 [16384], P(('dp', 'tensor')), may hold values from 0 to 3, as said below
- cotangent: bfloat16 [16384, 768], P(('dp', 'tensor')), may hold values from -6 to 6
- norm1_gain: float32 [768], replicated, may hold values from 0.1 to 1.9
- norm1_shift: float32 [768], replicated, may hold values from -1.75 to 1.75
- qkv_weight: bfloat16 [768, 3, 768], P(None, None, 'tensor'), may hold values from -0.3125 to 0.3125
- conv_kernel: float32 [3, 3, 768], P(None, None, 'tensor'), may hold values from -3.5 to 3.5
- out_weight: bfloat16 [768, 768], P('tensor'), may hold values from -0.875 to 0.875
- out_bias: float32 [768], replicated, may hold values from -1.75 to 1.75
- norm2_gain: float32 [768], replicated, may hold values from 0.1 to 1.9
- norm2_shift: float32 [768], replicated, may hold values from -1.75 to 1.75
- up_weight: bfloat16 [768, 3072], P(None, 'tensor'), may hold values from -0.21875 to 0.21875
- up_bias: float32 [3072], P('tensor'), may hold values from -3 to 3
- down_weight: bfloat16 [3072, 768], P('tensor'), may hold values from -0.109375 to 0.109375
- down_bias: float32 [768], replicated, may hold values from -1.75 to 1.75
Outputs:
- result: bfloat16 [16384, 768], P(('dp', 'tensor'))
- grad_tokens: float32 [16384, 768], P(('dp', 'tensor'))
- grad_norm1_gain: float32 [768], replicated
- grad_norm1_shift: float32 [768], replicated
- grad_qkv_weight: float32 [768, 3, 768], P(None, None, 'tensor')
- grad_conv_kernel: float32 [3, 3, 768], P(None, None, 'tensor')
- grad_out_weight: float32 [768, 768], P('tensor')
- grad_out_bias: float32 [768], replicated
- grad_norm2_gain: float32 [768], replicated
- grad_norm2_shift: float32 [768], replicated
- grad_up_weight: float32 [768, 3072], P(None, 'tensor')
- grad_up_bias: float32 [3072], P('tensor')
- grad_down_weight: float32 [3072, 768], P('tensor')
- grad_down_bias: float32 [768], replicated
Inputs may be any that keep to these rules, and one draw needn't show every extreme that they name: `segment_ids`: each sequence of 2048 tokens holds four documents numbered 0, 1, 2, 3 in order, each of one token or more.
All inputs are finite; a program needn't handle non-finite values.
Results may differ from a plain program's by a relative error of at most 0.02.
The roundings to bfloat16 on the way count: a program that leaves them out, or rounds other values in their place, can miss the bound.
Values may be sent and summed in bfloat16 or wider, within the bound.
A program may use at most 128 MiB of HBM per device.

v0:
```python
import jax
import jax.numpy as jnp
from jax import lax
from jax.sharding import PartitionSpec as P

HD = 64
LEN = 2048


EPS = 1e-05


def layer_norm(values, scale_gain, offset_shift):
    average = jnp.mean(values, -1, keepdims=True)
    centred = values - average
    inverse = lax.rsqrt(jnp.mean(centred * centred, -1, keepdims=True) + EPS)
    unit_rows = centred * inverse
    return (unit_rows * scale_gain + offset_shift, unit_rows, inverse)


def norm_back(gradient, unit_rows, inverse, scale_gain):
    scaled = gradient * scale_gain
    centred_grad = (
        scaled
        - jnp.mean(scaled, -1, keepdims=True)
        - unit_rows * jnp.mean(scaled * unit_rows, -1, keepdims=True)
    )
    return (centred_grad * inverse, jnp.sum(gradient * unit_rows, 0), jnp.sum(gradient, 0))


def outer_sum(left, right):
    return lax.dot_general(
        left, right, (((0,), (0,)), ((), ())), preferred_element_type=jnp.float32
    )


def times_transposed(left, right):
    return lax.dot_general(
        left, right, (((1,), (1,)), ((), ())), preferred_element_type=jnp.float32
    )


def shift_down(values, shift_lag):
    padding = jnp.zeros((shift_lag,) + values.shape[1:], values.dtype)
    return jnp.concatenate([padding, values[:-shift_lag]], 0)


def shift_up(values, shift_lag):
    padding = jnp.zeros((shift_lag,) + values.shape[1:], values.dtype)
    return jnp.concatenate([values[shift_lag:], padding], 0)


def conv_masks(seg_all):
    position = jnp.arange(seg_all.shape[0], dtype=jnp.int32) % LEN
    keep_masks = []
    for shift_lag in (1, 2):
        earlier_ids = shift_down(seg_all, shift_lag)
        keep_masks.append(
            ((position >= shift_lag) & (earlier_ids == seg_all)).astype(jnp.float32)[:, None, None]
        )
    return keep_masks


def mixing(projected, kernel, keep_masks):
    convolved = kernel[0] * projected
    for shift_lag in (1, 2):
        convolved = (
            convolved
            + kernel[shift_lag] * shift_down(projected, shift_lag) * keep_masks[shift_lag - 1]
        )
    return convolved


def mixing_back(grad_mixed, projected, kernel, keep_masks):
    kernel_rows = [jnp.sum(grad_mixed * projected, 0)]
    grad_proj = kernel[0] * grad_mixed
    for shift_lag in (1, 2):
        kept_grad = grad_mixed * keep_masks[shift_lag - 1]
        kernel_rows.append(jnp.sum(kept_grad * shift_down(projected, shift_lag), 0))
        grad_proj = grad_proj + shift_up(kernel[shift_lag] * kept_grad, shift_lag)
    return (grad_proj, jnp.stack(kernel_rows, 0))


def split_heads(convolved):
    group_rows = convolved.shape[0]
    local_width = convolved.shape[2]
    low_mixed = convolved.astype(jnp.bfloat16)
    return tuple(
        (
            low_mixed[:, which_one].reshape(group_rows, local_width // HD, HD)
            for which_one in range(3)
        )
    )


def block_scores(query_block, key_rows, seg_all, row_start, seq_start, block):
    query_pos = row_start + jnp.arange(block, dtype=jnp.int32)
    key_pos = seq_start + jnp.arange(LEN, dtype=jnp.int32)
    query_ids = lax.dynamic_slice_in_dim(seg_all, row_start, block, 0)
    allowed = (query_pos[:, None] >= key_pos[None, :]) & (query_ids[:, None] == seg_all[None, :])
    scores = jnp.einsum(
        "qhd,khd->hqk", query_block, key_rows, preferred_element_type=jnp.float32
    ) * float(HD) ** (-0.5)
    return jnp.where(allowed[None], scores, -1e30)


def attention(queries, key_all, value_all, seg_all):
    block = min(512, LEN)

    def one_block(block_index):
        row_start = block_index * block
        seq_start = row_start // LEN * LEN
        query_block = lax.dynamic_slice_in_dim(queries, row_start, block, 0)
        scores = block_scores(query_block, key_all, seg_all, row_start, seq_start, block)
        row_max = jnp.max(scores, -1, keepdims=True)
        exps = jnp.exp(scores - row_max)
        row_total = jnp.sum(exps, -1, keepdims=True)
        probabilities = (exps / row_total).astype(jnp.bfloat16)
        attended = jnp.einsum(
            "hqk,khd->qhd", probabilities, value_all, preferred_element_type=jnp.float32
        )
        return (attended, (row_max + jnp.log(row_total))[..., 0])

    attended, log_totals = lax.map(
        one_block, jnp.arange(queries.shape[0] // block, dtype=jnp.int32)
    )
    return (attended.reshape(queries.shape[0], -1), log_totals)


def attention_back(queries, key_all, value_all, seg_all, log_totals, grad_att):
    block = min(512, LEN)
    scaling = float(HD) ** (-0.5)
    zero_rows = jnp.zeros(queries.shape, jnp.float32)

    def one_block(block_index, state_tuple):
        grad_q, grad_k, grad_v = state_tuple
        row_start = block_index * block
        seq_start = row_start // LEN * LEN
        query_block = lax.dynamic_slice_in_dim(queries, row_start, block, 0)
        scores = block_scores(query_block, key_all, seg_all, row_start, seq_start, block)
        probabilities = jnp.exp(scores - log_totals[block_index][..., None])
        low_probs = probabilities.astype(jnp.bfloat16)
        grad_block = lax.dynamic_slice_in_dim(grad_att, row_start, block, 0)
        grad_probs = jnp.einsum(
            "qhd,khd->hqk", grad_block, value_all, preferred_element_type=jnp.float32
        )
        row_inner = jnp.sum(probabilities * grad_probs, -1, keepdims=True)
        grad_scores = (probabilities * (grad_probs - row_inner)).astype(jnp.bfloat16)
        query_grad = (
            jnp.einsum("hqk,khd->qhd", grad_scores, key_all, preferred_element_type=jnp.float32)
            * scaling
        )
        key_grad = (
            jnp.einsum("hqk,qhd->khd", grad_scores, query_block, preferred_element_type=jnp.float32)
            * scaling
        )
        value_grad = jnp.einsum(
            "hqk,qhd->khd", low_probs, grad_block, preferred_element_type=jnp.float32
        )
        grad_q = lax.dynamic_update_slice_in_dim(grad_q, query_grad, row_start, 0)
        grad_k = grad_k + key_grad
        grad_v = grad_v + value_grad
        return (grad_q, grad_k, grad_v)

    return lax.fori_loop(0, queries.shape[0] // block, one_block, (zero_rows, zero_rows, zero_rows))


def ffn_backward(gathered_two, gathered_grad, hidden, active, up_weight, down_weight):
    grad_act = times_transposed(gathered_grad, down_weight)
    grad_hidden = (grad_act * 2.0 * jax.nn.relu(hidden)).astype(jnp.bfloat16)
    grad_up = outer_sum(gathered_two, grad_hidden)
    grad_upb = jnp.sum(grad_hidden.astype(jnp.float32), 0)
    grad_down = outer_sum(active, gathered_grad)
    grad_second = lax.psum_scatter(
        times_transposed(grad_hidden, up_weight), "tensor", scatter_dimension=0, tiled=True
    )
    return (grad_up, grad_upb, grad_down, grad_second)


def per_device(
    tokens,
    segment_ids,
    cotangent,
    norm1_gain,
    norm1_shift,
    qkv_weight,
    conv_kernel,
    out_weight,
    out_bias,
    norm2_gain,
    norm2_shift,
    up_weight,
    up_bias,
    down_weight,
    down_bias,
):
    width = tokens.shape[1]
    local_width = qkv_weight.shape[2]
    qkv_flat = qkv_weight.reshape(width, 3 * local_width)
    inputs = tokens.astype(jnp.float32)
    normed_one, unit_one, inverse_one = layer_norm(inputs, norm1_gain, norm1_shift)
    normed_low = normed_one.astype(jnp.bfloat16)
    gathered_one, seg_all = (
        lax.all_gather(normed_low, "tensor", axis=0, tiled=True),
        lax.all_gather(segment_ids, "tensor", axis=0, tiled=True),
    )
    group_rows = gathered_one.shape[0]
    projected = jnp.dot(gathered_one, qkv_flat, preferred_element_type=jnp.float32).reshape(
        group_rows, 3, local_width
    )
    keep_masks = conv_masks(seg_all)
    queries, key_all, value_all = split_heads(mixing(projected, conv_kernel, keep_masks))
    attended, log_totals = attention(queries, key_all, value_all, seg_all)
    att_low = attended.astype(jnp.bfloat16)
    branch = lax.psum_scatter(
        jnp.dot(att_low, out_weight, preferred_element_type=jnp.float32),
        "tensor",
        scatter_dimension=0,
        tiled=True,
    )
    middle = inputs + branch + out_bias
    normed_two, unit_two, inverse_two = layer_norm(middle, norm2_gain, norm2_shift)
    second_low = normed_two.astype(jnp.bfloat16)
    grad_out = cotangent.astype(jnp.float32)
    gathered_two = lax.all_gather(second_low, "tensor", axis=0, tiled=True)
    hidden = jnp.dot(gathered_two, up_weight, preferred_element_type=jnp.float32) + up_bias
    active = jnp.square(jax.nn.relu(hidden)).astype(jnp.bfloat16)
    ffn_out = lax.psum_scatter(
        jnp.dot(active, down_weight, preferred_element_type=jnp.float32).astype(jnp.bfloat16),
        "tensor",
        scatter_dimension=0,
        tiled=True,
    ).astype(jnp.float32)
    result = (middle + ffn_out + down_bias).astype(jnp.bfloat16)
    gathered_grad = lax.all_gather(cotangent, "tensor", axis=0, tiled=True)
    grad_up, grad_upb, grad_down, grad_second = ffn_backward(
        gathered_two, gathered_grad, hidden, active, up_weight, down_weight
    )
    grad_mid_part, grad_gain_two, grad_shift_two = norm_back(
        grad_second, unit_two, inverse_two, norm2_gain
    )
    grad_middle = grad_out + grad_mid_part
    grad_outb = jnp.sum(grad_middle, 0)
    grad_downb = jnp.sum(grad_out, 0)
    branch_grad_all = lax.all_gather(grad_middle.astype(jnp.bfloat16), "tensor", axis=0, tiled=True)
    grad_outw = outer_sum(att_low, branch_grad_all)
    grad_att = (
        times_transposed(branch_grad_all, out_weight)
        .astype(jnp.bfloat16)
        .reshape(group_rows, local_width // HD, HD)
    )
    source_rows = lax.all_gather(normed_low, "tensor", axis=0, tiled=True)
    source_proj = jnp.dot(source_rows, qkv_flat, preferred_element_type=jnp.float32).reshape(
        group_rows, 3, local_width
    )
    again_q, again_k, again_v = split_heads(mixing(source_proj, conv_kernel, keep_masks))
    grad_q, grad_k, grad_v = attention_back(
        again_q, again_k, again_v, seg_all, log_totals, grad_att
    )
    grad_mixed = jnp.stack(
        [
            grad_q.reshape(group_rows, local_width),
            grad_k.reshape(group_rows, local_width),
            grad_v.reshape(group_rows, local_width),
        ],
        1,
    )
    grad_proj, grad_kernel = mixing_back(grad_mixed, source_proj, conv_kernel, keep_masks)
    grad_proj_low = grad_proj.astype(jnp.bfloat16).reshape(group_rows, 3 * local_width)
    grad_qkv = outer_sum(source_rows, grad_proj_low).reshape(width, 3, local_width)
    grad_first = lax.psum_scatter(
        times_transposed(grad_proj_low, qkv_flat).astype(jnp.bfloat16),
        "tensor",
        scatter_dimension=0,
        tiled=True,
    ).astype(jnp.float32)
    grad_in_part, grad_gain_one, grad_shift_one = norm_back(
        grad_first, unit_one, inverse_one, norm1_gain
    )
    grad_tokens = grad_middle + grad_in_part
    summed_w = lax.psum((grad_qkv, grad_kernel, grad_outw, grad_up, grad_upb, grad_down), "dp")
    summed_s = lax.psum(
        (grad_gain_one, grad_shift_one, grad_outb, grad_gain_two, grad_shift_two, grad_downb),
        ("dp", "tensor"),
    )
    return (
        result,
        grad_tokens,
        summed_s[0],
        summed_s[1],
        summed_w[0],
        summed_w[1],
        summed_w[2],
        summed_s[2],
        summed_s[3],
        summed_s[4],
        summed_w[3],
        summed_w[4],
        summed_w[5],
        summed_s[5],
    )


def solution(mesh):
    return jax.shard_map(
        per_device,
        mesh=mesh,
        in_specs=(
            P(("dp", "tensor"), None),
            P(("dp", "tensor")),
            P(("dp", "tensor"), None),
            P(),
            P(),
            P(None, None, "tensor"),
            P(None, None, "tensor"),
            P("tensor", None),
            P(),
            P(),
            P(),
            P(None, "tensor"),
            P("tensor"),
            P("tensor", None),
            P(),
        ),
        out_specs=(
            P(("dp", "tensor"), None),
            P(("dp", "tensor"), None),
            P(),
            P(),
            P(None, None, "tensor"),
            P(None, None, "tensor"),
            P("tensor", None),
            P(),
            P(),
            P(),
            P(None, "tensor"),
            P("tensor"),
            P("tensor", None),
            P(),
        ),
        check_vma=False,
    )
```

profile of v0, /device:TPU:0, one launch (start us, length us, event | category | flops | bytes accessed | tf_op | source)
XLA Modules:
  0.0 1043.3 jit_solution(2772871329400378792)
XLA Ops:
  13.3 13.6 %all-gather = s32[4,1,512]{2,1,0:T(1,128)S(1)} all-gather(s32[1,1,512]{2,1,0:T(1,128)S(1)} %bitcast.144), channel_id=1, replica_groups=mesh['dp'=8,'tensor'=4] {'tensor'}, dimensions={0}, use_global_device_ids=true | all-gather | bytes 10240 | tf_op jit(solution)/shard_map/all_gather | solution.py:205
  27.0 52.6 %all-gather.6.cloned.1.call-done = bf16[2048,768]{1,0:T(8,128)(2,1)} async-done(((bf16[512,768]{1,0:T(8,128)(2,1)}), bf16[2048,768]{1,0:T(8,128)(2,1)}) %all-gather.6.cloned.1.call-update) | async-done | bytes 3145744 | tf_op jit(solution)/shard_map/all_gather | solution.py:204
  79.6 3.9 fusion.71
  83.6 3.6 add_convert_fusion.1
  87.6 90.8 %while.34 = (s32[]{:T(128)}, bf16[4,512,3,64]{1,3,2,0:T(8,128)(2,1)}, f32[4,3,512]{2,1,0:T(4,128)}, s32[4]{0:T(128)S(1)}, s32[2048]{0:T(1024)S(1)}, /*index=5*/b...) while((s32[]{:T(128)}, ...), condition=%wide.region_5.6_spmd, body=%wide.region_2.5_spmd.sunk | while | flops 846201856 | bytes 50487736 | solution.py:124
  89.8 6.0 fusion.124
  95.8 6.8 fusion.125
  102.7 6.7 fusion.126
  112.5 6.0 fusion.124
  118.5 6.8 fusion.125
  125.4 6.7 fusion.126
  135.2 6.0 fusion.124
  141.2 6.8 fusion.125
  148.0 6.7 fusion.126
  157.9 6.0 fusion.124
  163.9 6.8 fusion.125
  170.7 6.7 fusion.126
  181.5 3.7 fusion.72
  185.6 109.2 %reduce-scatter.5.cloned.1.call-done = f32[512,768]{1,0:T(8,128)} async-done(((f32[2048,768]{1,0:T(8,128)}), f32[512,768]{1,0:T(8,128)}) %reduce-scatter.5.cloned.1.call-update) | async-done | bytes 1572880 | tf_op jit(solution)/shard_map/reduce_scatter | solution.py:215
  299.5 63.5 %all-gather.8.cloned.1.call-done = bf16[2048,768]{1,0:T(8,128)(2,1)} async-done(((bf16[512,768]{1,0:T(8,128)(2,1)}), bf16[2048,768]{1,0:T(8,128)(2,1)}) %all-gather.8.cloned.1.call-update) | async-done | bytes 3145744 | tf_op jit(solution)/shard_map/all_gather | solution.py:225
  363.1 7.5 fusion.73
  370.6 56.1 %all-gather.10.cloned.1.call-done = bf16[2048,768]{1,0:T(8,128)(2,1)} async-done(((bf16[512,768]{1,0:T(8,128)(2,1)}), bf16[2048,768]{1,0:T(8,128)(2,1)}) %all-gather.10.cloned.1.call-update) | async-done | bytes 3145744 | tf_op jit(solution)/shard_map/all_gather | solution.py:235
  426.7 7.4 convert_reduce_fusion
  435.7 4.5 fusion.74
  440.3 7.1 convolution_convert_fusion
  447.5 102.3 %reduce-scatter.9.cloned.1.call-done = f32[512,768]{1,0:T(8,128)} async-done(((f32[2048,768]{1,0:T(8,128)}), f32[512,768]{1,0:T(8,128)}) %reduce-scatter.9.cloned.1.call-update) | async-done | bytes 1572880 | tf_op jit(solution)/shard_map/reduce_scatter | solution.py:174
  549.8 3.2 multiply_reduce_fusion.4
  553.0 59.8 %reduce-scatter.7.cloned.1.call-done = bf16[512,768]{1,0:T(8,128)(2,1)} async-done(((bf16[2048,768]{1,0:T(8,128)(2,1)}), bf16[512,768]{1,0:T(8,128)(2,1)}) %reduce-scatter.7.cloned.1.call-update) | async-done | bytes 786448 | tf_op jit(solution)/shard_map/reduce_scatter | solution.py:228
  612.8 4.4 fusion.67
  619.4 63.6 %all-gather.12.cloned.1.call-done = bf16[2048,768]{1,0:T(8,128)(2,1)} async-done(((bf16[512,768]{1,0:T(8,128)(2,1)}), bf16[2048,768]{1,0:T(8,128)(2,1)}) %all-gather.12.cloned.1.call-update) | async-done | bytes 3145744 | tf_op jit(solution)/shard_map/all_gather | solution.py:245
  683.0 3.1 convolution_convert_fusion.1
  687.4 143.7 %while.35 = (s32[]{:T(128)}, f32[2048,3,64]{0,2,1:T(8,128)}, f32[2048,3,64]{0,2,1:T(8,128)}, f32[2048,3,64]{0,2,1:T(8,128)}, s32[2048]{0:T(1024)S(1)}, /*index=5...) while((s32[]{:T(128)}, f32[2048,3,64]{0,2,1:T(8,128)}, ...), condition=%wide.region_15.16_spmd.clone, body=%wide.region_13.15_spmd.clone.sunk | while | flops 2065662976 | bytes 144128688 | solution.py:165
  702.0 4.7 fusion.139
  706.7 5.8 multiply_reduce_fusion.9
  712.5 6.5 multiply_convert_fusion.6
  719.0 4.4 fusion.138
  723.4 6.2 fusion.137
  731.4 3.0 fusion.136
  734.4 6.1 fusion.139
  740.5 5.8 multiply_reduce_fusion.9
  746.3 6.5 multiply_convert_fusion.6
  752.7 4.4 fusion.138
  757.2 6.2 fusion.137
  768.2 6.1 fusion.139
  774.3 5.8 multiply_reduce_fusion.9
  780.1 6.5 multiply_convert_fusion.6
  786.5 4.4 fusion.138
  790.9 6.2 fusion.137
  802.0 6.1 fusion.139
  808.1 5.8 multiply_reduce_fusion.9
  813.8 6.5 multiply_convert_fusion.6
  820.3 4.4 fusion.138
  824.7 6.2 fusion.137
  831.1 7.4 multiply_reduce_fusion.2
  841.9 4.3 pad_maximum_fusion
  847.6 4.0 bitcast_convert_fusion
  851.7 7.1 fusion.76
  858.8 7.0 fusion.55
  867.5 3.3 fusion.36
  870.9 4.5 multiply_reduce_fusion.3
  875.4 25.3 %all-reduce.6 = (f32[3,3,192]{2,1,0:T(4,128)}, f32[768]{0:T(1024)}) all-reduce(f32[3,3,192]{2,1,0:T(4,128)S(1)} %pad_maximum_fusion.1, f32[768]{0:T(1024)S(1)} %copy-done.59), channel_id=1, replica_groups=mesh['dp'=8,'tensor'=4] {'dp'}, use_global_device_ids=true, to_apply=%region_27.28 | all-reduce | flops 2496 | bytes 19968 | tf_op jit(solution)/shard_map/psum | solution.py:281
  900.8 9.9 reduce-scatter.11.cloned.1.call-done
  912.7 41.5 %all-reduce.5 = (f32[768]{0:T(1024)}, f32[768]{0:T(1024)}, f32[768]{0:T(1024)}, f32[768]{0:T(1024)}, f32[768]{0:T(1024)}, /*index=5*/f32[768]{0:T(1024)}) all-reduce(f32[768]{0:T(1024)S(1)} %get-tuple-element.403, f32[768]{0:T(1024)S(1)} %get-tuple-element.407, ...), channel_id=1, replica_groups=mesh['dp'=8,'tensor'=4] {'dp','tensor'}, use_global_device_ids=true, to_apply=%region_20.21 | all-reduce | flops 4608 | bytes 36864 | tf_op jit(solution)/shard_map/psum | solution.py:282
  957.0 72.7 %all-reduce.10.cloned.1.call-done = (f32[768,3,192]{0,2,1:T(8,128)}, f32[192,768]{1,0:T(8,128)}, f32[768,768]{1,0:T(8,128)}, f32[768,768]{1,0:T(8,128)}) async-done(((f32[768,3,192]{0,2,1:T(8,128)}, f32[192,768]{1,0:T(8,128)}, f32[768,768]{1,0:T(8,128)}, f32[768,768]{1,0:T(8,128)}), (f32[768,3,192]{0,2,1:T(8,128)}, f32[192,768]{1,0:T(8,128)}, f32[768,768]{1,0:T(8,128)}, ...) | async-done | bytes 7077904 | tf_op jit(solution)/shard_map/psum | solution.py:281
  (299 shorter events, 63.7 us)
Async XLA Ops:
  7.2 419.5 %copy-start = (bf16[768,768]{1,0:T(8,128)(2,1)S(1)}, bf16[768,768]{1,0:T(8,128)(2,1)}, u32[]{:S(2)}) copy-start(bf16[768,768]{1,0:T(8,128)(2,1)} %param.32) | copy-start | bytes 3538948
  7.2 6.1 copy-start.60
  7.2 19.7 %copy-start.56 = (f32[3,3,192]{2,1,0:T(4,128)S(1)}, f32[3,3,192]{2,1,0:T(4,128)}, u32[]{:S(2)}) copy-start(f32[3,3,192]{2,1,0:T(4,128)} %param.25) | copy-start | bytes 20740
  7.2 72.4 %copy-start.63 = (bf16[768,3,192]{0,2,1:T(8,128)(2,1)S(1)}, bf16[768,3,192]{0,2,1:T(8,128)(2,1)}, u32[]{:S(2)}) copy-start(bf16[768,3,192]{0,2,1:T(8,128)(2,1)} %param.24) | copy-start | bytes 2654212
  7.2 72.4 %all-gather.6.cloned.1.call-start = ((), (), s32[]{:S(2)}) async-start(), calls=%async_computation.4 | async-start | bytes 3932160 | tf_op jit(solution)/shard_map/all_gather | solution.py:204
  13.2 281.6 %reduce-scatter.5.cloned.1.call-start = ((), (), s32[]{:S(2)}) async-start(), calls=%async_computation.5 | async-start | bytes 7864320 | tf_op jit(solution)/shard_map/reduce_scatter | solution.py:215
  26.9 56.7 %copy-start.43 = (f32[3,192]{1,0:T(4,128)}, f32[3,192]{1,0:T(4,128)S(1)}, u32[]{:S(2)}) copy-start(f32[3,192]{1,0:T(4,128)S(1)} %get-tuple-element.477) | copy-start | bytes 6916
  26.9 56.7 %copy-start.45 = (f32[3,192]{1,0:T(4,128)}, f32[3,192]{1,0:T(4,128)S(1)}, u32[]{:S(2)}) copy-start(f32[3,192]{1,0:T(4,128)S(1)} %get-tuple-element.478) | copy-start | bytes 6916
  26.9 56.7 %copy-start.47 = (f32[3,192]{1,0:T(4,128)}, f32[3,192]{1,0:T(4,128)S(1)}, u32[]{:S(2)}) copy-start(f32[3,192]{1,0:T(4,128)S(1)} %get-tuple-element.479) | copy-start | bytes 6916
  27.0 56.6 %copy-start.36 = (f32[2048]{0:T(1024)}, f32[2048]{0:T(1024)S(1)}, u32[]{:S(2)}) copy-start(f32[2048]{0:T(1024)S(1)} %get-tuple-element.480) | copy-start | bytes 24580
  27.0 56.6 %copy-start.38 = (f32[2048]{0:T(1024)}, f32[2048]{0:T(1024)S(1)}, u32[]{:S(2)}) copy-start(f32[2048]{0:T(1024)S(1)} %get-tuple-element.481) | copy-start | bytes 24580
  95.8 6.8 copy-start.29
  118.5 6.8 copy-start.29
  141.2 6.8 copy-start.29
  163.9 6.8 copy-start.29
  178.3 6.9 copy-start.19
  185.2 109.6 %copy-start.12 = (bf16[512,768]{1,0:T(8,128)(2,1)S(1)}, bf16[512,768]{1,0:T(8,128)(2,1)}, u32[]{:S(2)}) copy-start(bf16[512,768]{1,0:T(8,128)(2,1)} %param.19) | copy-start | bytes 2359300
  185.3 112.4 %copy-start.42 = (f32[768]{0:T(1024)S(1)}, f32[768]{0:T(1024)}, u32[]{:S(2)}) copy-start(f32[768]{0:T(1024)} %param.28) | copy-start | bytes 9220
  185.3 112.4 %copy-start.57 = (f32[768]{0:T(1024)S(1)}, f32[768]{0:T(1024)}, u32[]{:S(2)}) copy-start(f32[768]{0:T(1024)} %param.29) | copy-start | bytes 9220
  185.3 177.8 %all-gather.8.cloned.1.call-start = ((), (), s32[]{:S(2)}) async-start(), calls=%async_computation.6 | async-start | bytes 3932160 | tf_op jit(solution)/shard_map/all_gather | solution.py:225
  298.9 127.8 %all-gather.10.cloned.1.call-start = ((), (), s32[]{:S(2)}) async-start(), calls=%async_computation.8 | async-start | bytes 3932160 | tf_op jit(solution)/shard_map/all_gather | solution.py:235
  299.5 127.2 %copy-start.34 = (f32[768]{0:T(1024)S(1)}, f32[768]{0:T(1024)}, u32[]{:S(2)}) copy-start(f32[768]{0:T(1024)} %param.31) | copy-start | bytes 9220
  299.5 250.3 %reduce-scatter.9.cloned.1.call-start = ((), (), s32[]{:S(2)}) async-start(), calls=%async_computation.9 | async-start | bytes 7864320 | tf_op jit(solution)/shard_map/reduce_scatter | solution.py:174
  426.7 9.0 copy-start.62
  440.2 172.5 %reduce-scatter.7.cloned.1.call-start = ((), (), s32[]{:S(2)}) async-start(), calls=%async_computation.7 | async-start | bytes 3932160 | tf_op jit(solution)/shard_map/reduce_scatter | solution.py:228
  447.4 165.3 %copy-start.22 = (bf16[512,768]{1,0:T(8,128)(2,1)S(1)}, bf16[512,768]{1,0:T(8,128)(2,1)}, u32[]{:S(2)}) copy-start(bf16[512,768]{1,0:T(8,128)(2,1)} %param.21) | copy-start | bytes 2359300
  447.4 165.3 %copy-start.58 = (f32[768]{0:T(1024)S(1)}, f32[768]{0:T(1024)}, u32[]{:S(2)}) copy-start(f32[768]{0:T(1024)} %param.33) | copy-start | bytes 9220
  447.5 235.5 %all-gather.12.cloned.1.call-start = ((), (), s32[]{:S(2)}) async-start(), calls=%async_computation.10 | async-start | bytes 3932160 | tf_op jit(solution)/shard_map/all_gather | solution.py:245
  617.2 65.8 %copy-start.33 = (bf16[192,768]{1,0:T(8,128)(2,1)S(1)}, bf16[192,768]{1,0:T(8,128)(2,1)}, u32[]{:S(2)}) copy-start(bf16[192,768]{1,0:T(8,128)(2,1)} %param.26) | copy-start | bytes 884740
  619.3 291.4 %reduce-scatter.11.cloned.1.call-start = ((), (), s32[]{:S(2)}) async-start(), calls=%async_computation.11 | async-start | bytes 3932160 | tf_op jit(solution)/shard_map/reduce_scatter | solution.py:271
  687.4 143.7 %copy-start.37 = (f32[2048]{0:T(1024)S(1)}, f32[2048]{0:T(1024)}, u32[]{:S(2)}) copy-start(f32[2048]{0:T(1024)} %copy-done.36) | copy-start | bytes 24580
  687.4 143.7 %copy-start.39 = (f32[2048]{0:T(1024)S(1)}, f32[2048]{0:T(1024)}, u32[]{:S(2)}) copy-start(f32[2048]{0:T(1024)} %copy-done.38) | copy-start | bytes 24580
  712.5 6.5 copy-start.6
  723.3 6.2 copy-start.7
  723.3 6.2 copy-start.10
  723.4 6.2 copy-start.28
  746.3 6.5 copy-start.6
  757.1 6.2 copy-start.7
  757.1 6.2 copy-start.10
  757.1 6.2 copy-start.28
  780.0 6.5 copy-start.6
  790.9 6.2 copy-start.7
  790.9 6.2 copy-start.10
  790.9 6.2 copy-start.28
  813.8 6.5 copy-start.6
  824.7 6.2 copy-start.7
  824.7 6.2 copy-start.10
  824.7 6.2 copy-start.28
  831.1 7.4 copy-start.48
  851.7 7.1 copy-start.21
  851.7 7.1 copy-start.35
  851.7 178.1 %all-reduce.10.cloned.1.call-start = ((), (), s32[]{:S(2)}) async-start(), calls=%async_computation.12 | async-start | bytes 14155776 | tf_op jit(solution)/shard_map/psum | solution.py:281
  858.8 7.0 copy-start.18
  858.8 7.0 copy-start.20
  858.8 8.6 copy-start.61
  870.8 40.0 %copy-start.13 = (bf16[512,768]{1,0:T(8,128)(2,1)S(1)}, bf16[512,768]{1,0:T(8,128)(2,1)}, u32[]{:S(2)}) copy-start(bf16[512,768]{1,0:T(8,128)(2,1)} %param.19) | copy-start | bytes 2359300
  870.8 39.9 %copy-start.41 = (f32[512]{0:T(512)S(1)}, f32[512]{0:T(512)}, u32[]{:S(2)}) copy-start(f32[512]{0:T(512)} %copy-done.40) | copy-start | bytes 6148
  870.8 39.9 %copy-start.49 = (f32[768]{0:T(1024)S(1)}, f32[768]{0:T(1024)}, u32[]{:S(2)}) copy-start(f32[768]{0:T(1024)} %param.22) | copy-start | bytes 9220
  870.8 39.9 %copy-start.51 = (f32[512]{0:T(512)S(1)}, f32[512]{0:T(512)}, u32[]{:S(2)}) copy-start(f32[512]{0:T(512)} %copy-done.50) | copy-start | bytes 6148
  870.8 41.9 %copy-start.52 = (f32[768]{0:T(1024)S(1)}, f32[768]{0:T(1024)}, u32[]{:S(2)}) copy-start(f32[768]{0:T(1024)} %get-tuple-element.400) | copy-start | bytes 9220
  870.8 41.9 %copy-start.53 = (f32[768]{0:T(1024)S(1)}, f32[768]{0:T(1024)}, u32[]{:S(2)}) copy-start(f32[768]{0:T(1024)} %get-tuple-element.405) | copy-start | bytes 9220
  870.8 41.9 %copy-start.54 = (f32[768]{0:T(1024)S(1)}, f32[768]{0:T(1024)}, u32[]{:S(2)}) copy-start(f32[768]{0:T(1024)} %get-tuple-element.460) | copy-start | bytes 9220
  870.8 41.9 %copy-start.55 = (f32[768]{0:T(1024)S(1)}, f32[768]{0:T(1024)}, u32[]{:S(2)}) copy-start(f32[768]{0:T(1024)} %get-tuple-element.476) | copy-start | bytes 9220
  870.9 83.3 %copy-start.16 = (f32[512,768]{1,0:T(8,128)S(1)}, f32[512,768]{1,0:T(8,128)}, u32[]{:S(2)}) copy-start(f32[512,768]{1,0:T(8,128)} %copy-done.15) | copy-start | bytes 4718596
  (44 other events, 137.0 us)
Sparse Core Ops, SparseCore 0:
  13.4 66.1 all-gather.5
  185.4 109.3 reduce-scatter.4
  299.0 64.0 all-gather.7
  364.5 62.1 all-gather.9
  440.4 109.3 reduce-scatter.8
  552.0 60.7 reduce-scatter.6
  619.5 63.5 all-gather.11
  851.8 58.8 reduce-scatter.10
  915.6 114.1 all-reduce.9
where the time goes:
time: 1050 us; the launch traced here: 1040 us
  waiting for transfers between devices  590 us (56%)
  matrix products  211 us (20%)
  other arithmetic  108 us (10%)
  blocking collectives  80.3 us (8%)
  local copies, waits for them, and re-layouts  24.6 us (2%)
  between operations  14.8 us (1%)
  loops' own time  13.6 us (1%)
    reduce_scatter x1, waiting for transfers between devices, per_device(): lax.psum_scatter(jnp.dot(att_low, out_weight, preferred_element_type=jnp....  109 us
    reduce_scatter x1, waiting for transfers between devices, ffn_backward(): lax.psum_scatter(times_transposed(grad_hidden, up_weight), 'tensor', scat...  102 us
    psum x1, waiting for transfers between devices, per_device(): lax.psum((grad_qkv, grad_kernel, grad_outw, grad_up, grad_upb, grad_down)...  72.7 us
    all_gather x1, waiting for transfers between devices, per_device(): lax.all_gather(grad_middle.astype(jnp.bfloat16), 'tensor', axis=0, tiled=...  63.6 us
    all_gather x1, waiting for transfers between devices, per_device(): gathered_two = lax.all_gather(second_low, 'tensor', axis=0, tiled=True)  63.5 us
    reduce_scatter x1, waiting for transfers between devices, per_device(): lax.psum_scatter(jnp.dot(active, down_weight, preferred_element_type=jnp....  59.8 us
    all_gather x1, waiting for transfers between devices, per_device(): gathered_grad = lax.all_gather(cotangent, 'tensor', axis=0, tiled=True)  56.1 us
    all_gather x1, waiting for transfers between devices, per_device(): lax.all_gather(normed_low, 'tensor', axis=0, tiled=True)  52.6 us
  transfers between devices with their start and end apart: 9, of which 9 were waited for; matrix products, arithmetic and copies ran while one was open for 4% of the time, Pallas kernels for 0%

commit v1 on v0

v1 whole, which is shorter than its diff:
```python
import functools
import jax, jax.numpy as jnp
from jax import lax
from jax.experimental import pallas as pl
from jax.experimental.pallas import tpu as pltpu
from jax.sharding import PartitionSpec as P_

HD=64
BF=jnp.bfloat16; F32=jnp.float32
BIG=1e30
def nt(a,b): return lax.dot_general(a,b,(((1,),(1,)),((),())),preferred_element_type=F32)
def tn(a,b): return lax.dot_general(a,b,(((0,),(0,)),((),())),preferred_element_type=F32)
def nn(a,b): return jnp.dot(a,b,preferred_element_type=F32)

def keep_rows(ids):
    n=ids.shape[1]
    pos=lax.broadcasted_iota(jnp.int32,(1,n),1)
    out=[]
    for j in (1,2):
        prev=pltpu.roll(ids,j,1)
        out.append(jnp.where((prev==ids)&(pos>=j),1.0,0.0).astype(F32))
    return out

def mix(v,ck,keeps,r):
    out=ck[r:r+HD,0:1]*v
    for j in (1,2):
        out=out+ck[r:r+HD,j:j+1]*(pltpu.roll(v,j,1)*keeps[j-1])
    return out

def feats(ids,rows,kind):
    n=ids.shape[1]
    r=lax.broadcasted_iota(jnp.int32,(rows,n),0)
    idb=jnp.broadcast_to(ids,(rows,n))
    if kind=="q":
        return jnp.where((r<4)&(idb!=r),-BIG,0.0).astype(F32)
    return jnp.where(((r<4)&(idb==r))|((r>=4)&(r<7)),1.0,0.0).astype(F32)

def fwd_kernel(n,heads,bq,x_ref,wt_ref,ck_ref,ids_ref, att_ref,proj_ref,lse_ref,of_ref, qt,kk,vt):
    for s in range(0,n,512):
        proj_ref[:,s:s+512]=nt(wt_ref[...],x_ref[s:s+512,:])
    ids=ids_ref[...]
    keeps=keep_rows(ids)
    fq=feats(ids,64,"q").astype(BF); fk=feats(ids,64,"k")
    lw=heads*HD
    ck=ck_ref[...]
    for h in range(heads):
        r=h*HD
        q=mix(proj_ref[r:r+HD,:],ck,keeps,r)
        qt[h,0:64,:]=(q.astype(BF).astype(F32)*0.125).astype(BF)
        qt[h,64:128,:]=fq
        r=lw+h*HD
        k=mix(proj_ref[r:r+HD,:],ck,keeps,r)
        kt=jnp.concatenate([k,fk],0)
        kk[h]=kt.T.astype(BF)
        r=2*lw+h*HD
        v=mix(proj_ref[r:r+HD,:],ck,keeps,r)
        vt[h,0:64,:]=v.astype(BF)
        vt[h,64:80,:]=jnp.ones((16,n),BF)
    tri=lax.broadcasted_iota(jnp.int32,(bq,bq),0)<=lax.broadcasted_iota(jnp.int32,(bq,bq),1)
    def head(h,_):
        for iq in range(n//bq):
            qs=iq*bq
            qb=qt[h,:,qs:qs+bq]
            ss=[]
            for j in range(iq+1):
                s=nn(kk[h,j*bq:(j+1)*bq,:],qb)
                if j==iq: s=jnp.where(tri,s,-BIG)
                ss.append(s)
            m=jnp.max(ss[0],axis=0,keepdims=True)
            for s in ss[1:]: m=jnp.maximum(m,jnp.max(s,axis=0,keepdims=True))
            o=jnp.zeros((80,bq),F32)
            for j,s in enumerate(ss):
                p=jnp.exp(s-m).astype(BF)
                o=o+nn(vt[h,:,j*bq:(j+1)*bq],p)
            l=o[64:65,:]
            of=o[0:64,:]/l
            rr=pl.multiple_of(h*HD,HD)
            of_ref[pl.ds(rr,HD),qs:qs+bq]=of
            att_ref[qs//512,pl.ds(rr,HD),qs%512:qs%512+bq]=of.astype(BF)
            lse_ref[h,:,qs:qs+bq]=jnp.broadcast_to(m+jnp.log(l),(8,bq))
        return 0
    lax.fori_loop(0,heads,head,0)

def attn_fwd(x,wt,ck,ids,bq=256):
    n,heads=x.shape[0],wt.shape[0]//3//HD
    lw=heads*HD
    vm=pl.BlockSpec(memory_space=pltpu.VMEM)
    return pl.pallas_call(
        functools.partial(fwd_kernel,n,heads,bq),
        out_shape=(jax.ShapeDtypeStruct((n//512,lw,512),BF),jax.ShapeDtypeStruct((3*lw,n),F32),jax.ShapeDtypeStruct((heads,8,n),F32),jax.ShapeDtypeStruct((lw,n),F32)),
        in_specs=[vm]*4,out_specs=(vm,)*4,
        scratch_shapes=[pltpu.VMEM((heads,128,n),BF),pltpu.VMEM((heads,n,128),BF),pltpu.VMEM((heads,80,n),BF)],
        compiler_params=pltpu.CompilerParams(vmem_limit_bytes=60*2**20),
    )(x,wt,ck,ids)

def split3(x):
    hi=x.astype(BF).astype(F32); r=x-hi; mid=r.astype(BF).astype(F32); lo=r-mid
    return hi,mid,lo

def bwd_kernel(n,heads,B,x_ref,wt_ref,ck_ref,ids_ref,proj_ref,lse_ref,of_ref,ga_ref, gf_ref,gw_ref,gc_ref, qt,qn,kk,kt_s,vn,dot_s,don,dq,dkv,gconv,gp):
    ids=ids_ref[...]
    keeps=keep_rows(ids)
    fq=feats(ids,64,"q"); fk=feats(ids,64,"k")
    r8=lax.broadcasted_iota(jnp.int32,(64,n),0)
    lw=heads*HD
    ck=ck_ref[...]
    zl=jnp.zeros((64,n),F32)
    for h in range(heads):
        r=h*HD
        q=mix(proj_ref[r:r+HD,:],ck,keeps,r).astype(BF).astype(F32)*0.125
        hi,mid,lo=split3(-lse_ref[h,0:1,:])
        f=fq+jnp.where(r8==4,hi,0.0)+jnp.where(r8==5,mid,0.0)+jnp.where(r8==6,lo,0.0)
        qt[h,0:64,:]=q.astype(BF); qt[h,64:128,:]=f.astype(BF)
        qn[h]=jnp.concatenate([zl,q],0).T.astype(BF)
        r=lw+h*HD
        k=mix(proj_ref[r:r+HD,:],ck,keeps,r)
        kt_s[h]=k.astype(BF)
        kk[h]=jnp.concatenate([k,fk],0).T.astype(BF)
        r=2*lw+h*HD
        v=mix(proj_ref[r:r+HD,:],ck,keeps,r)
        vn[h]=jnp.concatenate([v,jnp.where(r8<3,1.0,0.0)],0).T.astype(BF)
        do=jnp.concatenate([ga_ref[s,h*HD:(h+1)*HD,:] for s in range(n//512)],axis=1).astype(F32)
        D=jnp.sum(do*of_ref[h*HD:(h+1)*HD,:],axis=0,keepdims=True)
        hi,mid,lo=split3(-D)
        f=jnp.where(r8==0,hi,0.0)+jnp.where(r8==1,mid,0.0)+jnp.where(r8==2,lo,0.0)
        dot_s[h,0:64,:]=do.astype(BF); dot_s[h,64:128,:]=f.astype(BF)
        don[h]=jnp.concatenate([do,zl],0).T.astype(BF)
    tri=lax.broadcasted_iota(jnp.int32,(B,B),0)<=lax.broadcasted_iota(jnp.int32,(B,B),1)
    nb=n//B
    def head(h,_):
        for j in range(nb):
            js=j*B
            acc=jnp.zeros((B,128),F32)
            for i in range(j,nb):
                s_=i*B
                st=nn(kk[h,js:js+B,:],qt[h,:,s_:s_+B])
                p=jnp.exp(st)
                if i==j: p=jnp.where(tri,p,0.0)
                dp=nn(vn[h,js:js+B,:],dot_s[h,:,s_:s_+B])
                ds=(p*dp).astype(BF)
                acc=acc+nn(p.astype(BF),don[h,s_:s_+B,:])+nn(ds,qn[h,s_:s_+B,:])
                t=nn(kt_s[h,:,js:js+B],ds)
                if j==0: dq[:,s_:s_+B]=t
                else: dq[:,s_:s_+B]+=t
            dkv[js:js+B,:]=acc
        r=pl.multiple_of(h*HD,HD)
        gconv[pl.ds(r,HD),:]=dq[...]*0.125
        tt=dkv[...].T
        gconv[pl.ds(pl.multiple_of(2*lw+h*HD,HD),HD),:]=tt[0:64]
        gconv[pl.ds(pl.multiple_of(lw+h*HD,HD),HD),:]=tt[64:128]
        return 0
    lax.fori_loop(0,heads,head,0)
    for b in range(3*heads):
        r=b*HD
        g=gconv[r:r+HD,:]
        pr=proj_ref[r:r+HD,:]
        cols=[jnp.sum(g*pr,axis=1,keepdims=True)]
        o=ck[r:r+HD,0:1]*g
        for jj in (1,2):
            kg=g*keeps[jj-1]
            cols.append(jnp.sum(kg*pltpu.roll(pr,jj,1),axis=1,keepdims=True))
            o=o+ck[r:r+HD,jj:jj+1]*pltpu.roll(kg,n-jj,1)
        gp[r:r+HD,:]=o.astype(BF)
        gc_ref[r:r+HD,:]=jnp.concatenate(cols,1)
    gw_ref[...]=nn(gp[...],x_ref[...]).astype(BF)
    for s in range(0,n,512):
        gf_ref[s:s+512,:]=tn(gp[:,s:s+512],wt_ref[...]).astype(BF)

def attn_bwd(x,wt,ck,ids,proj,lse,of,ga,B=256):
    n,heads=x.shape[0],wt.shape[0]//3//HD
    lw=heads*HD
    vm=pl.BlockSpec(memory_space=pltpu.VMEM)
    V=pltpu.VMEM
    return pl.pallas_call(
        functools.partial(bwd_kernel,n,heads,B),
        out_shape=(jax.ShapeDtypeStruct((n,768),BF),jax.ShapeDtypeStruct((3*lw,768),BF),jax.ShapeDtypeStruct((3*lw,3),F32)),
        in_specs=[vm]*8,out_specs=(vm,)*3,
        scratch_shapes=[V((heads,128,n),BF),V((heads,n,128),BF),V((heads,n,128),BF),V((heads,64,n),BF),V((heads,n,128),BF),V((heads,128,n),BF),V((heads,n,128),BF),V((64,n),F32),V((n,128),F32),V((3*lw,n),F32),V((3*lw,n),BF)],
        compiler_params=pltpu.CompilerParams(vmem_limit_bytes=60*2**20),
    )(x,wt,ck,ids,proj,lse,of,ga)
EPS=1e-5
def ln(x):
    mu=jnp.mean(x,-1,keepdims=True)
    c=x-mu
    inv=lax.rsqrt(jnp.mean(c*c,-1,keepdims=True)+EPS)
    return c*inv,inv
def ln_back(g,unit,inv,gain):
    s=g*gain
    return (s-jnp.mean(s,-1,keepdims=True)-unit*jnp.mean(s*unit,-1,keepdims=True))*inv
def ffn_kernel(att_ref,tok_ref,cot_ref,ow_ref,up_ref,dn_ref,outb,g2,s2,upb,dnb,
               res_ref,gm_ref,ga_ref,gow_ref,gup_ref,gdn_ref,small_ref,gupb_ref, sec,act,gh,gsec):
    T=up_ref.shape[0]
    unit_mid=tok_ref[...].astype(F32)+tn(att_ref[...],ow_ref[...])+outb[...]
    unit,inv=ln(unit_mid)
    sec[...]=(unit*g2[...]+s2[...]).astype(BF)
    cot=cot_ref[...]
    gsec[...]=jnp.zeros_like(gsec)
    def blk(b,_):
        rl=jnp.maximum(nn(sec[...],up_ref[b])+upb[pl.ds(b,1),:],0.0)
        act[b]=(rl*rl).astype(BF)
        g=(nt(cot,dn_ref[b])*(2.0*rl)).astype(BF)
        gh[b]=g
        gupb_ref[pl.ds(b,1),:]=jnp.sum(g.astype(F32),0,keepdims=True)
        gsec[...]+=nt(g,up_ref[b])
        return 0
    lax.fori_loop(0,T,blk,0)
    gs=gsec[...]
    cf=cot.astype(F32)
    gm=cf+ln_back(gs,unit,inv,g2[...])
    gm_ref[...]=gm
    gmb=gm.astype(BF)
    lw=ow_ref.shape[0]//T
    for m in range(T):
        ga_ref[m]=nt(ow_ref[m*lw:(m+1)*lw,:],gmb).astype(BF)
    small_ref[0:1]=jnp.sum(gm,0,keepdims=True)
    small_ref[1:2]=jnp.sum(gs*unit,0,keepdims=True)
    small_ref[2:3]=jnp.sum(gs,0,keepdims=True)
    small_ref[3:4]=jnp.sum(cf,0,keepdims=True)
    small_ref[4:8]=jnp.zeros((4,cf.shape[1]),F32)
    gow_ref[...]=nn(att_ref[...],gmb).astype(BF)
    gsec[...]=unit_mid+dnb[...]
    def blk2(b,_):
        gsec[...]+=nn(act[b],dn_ref[b])
        gup_ref[b]=tn(sec[...],gh[b]).astype(BF)
        gdn_ref[b]=tn(act[b],cot_ref[...]).astype(BF)
        return 0
    lax.fori_loop(0,T,blk2,0)
    res_ref[...]=gsec[...].astype(BF)

def ffn(att,tok,cot,ow,up,dn,outb,g2,s2,upb,dnb):
    n,D=tok.shape; T=up.shape[0]; lw=ow.shape[0]//T; fb=up.shape[2]
    vm=pl.BlockSpec(memory_space=pltpu.VMEM); V=pltpu.VMEM
    S=jax.ShapeDtypeStruct
    return pl.pallas_call(ffn_kernel,
        out_shape=(S((n,D),BF),S((n,D),F32),S((T,lw,n),BF),S(ow.shape,BF),S(up.shape,BF),S(dn.shape,BF),S((8,D),F32),S((T,fb),F32)),
        in_specs=[vm]*11,out_specs=(vm,)*8,
        scratch_shapes=[V((n,D),BF),V((T,n,fb),BF),V((T,n,fb),BF),V((n,D),F32)],
        compiler_params=pltpu.CompilerParams(vmem_limit_bytes=60*2**20),
    )(att,tok,cot,ow,up,dn,outb,g2,s2,upb,dnb)
MESH=pl.DeviceIdType.MESH

class Place:
    def __init__(self):
        d=lax.axis_index("dp"); t=lax.axis_index("tensor")
        self.d,self.t=d,t
        b=d%2; p=t//2; q=t%2; base=d-b
        self.b,self.p,self.q=b,p,q
        self.member=2*q+b
        self.quarter=(d//2)%4
        self.sib=(base+1-b,t)
        self.opp=(d,2*p+1-q)
        self.cross=(base+1-b,2*p+1-q)
        self.other=(d,2*(1-p)+q)
        self.dest=(base+q,2*b+p)
        self.source=(base+p,2*q+b)
        self.fixed=jnp.logical_and(b==p,b==q)
        dx=d+2-4*((d//2)%2); dy=d+4-8*((d//4)%2)
        self.x=(dx,t); self.y=(dy,t); self.xy=(dx+dy-d,t)
    def zed(self,r): return (self.d,(self.t+r)%4)
    def column(self):
        base=self.d-self.b
        out=[]
        for r in range(1,4):
            out.append((self.d,(self.t+r)%4))
        for r in range(4):
            out.append((base+1-self.b,(self.t+r)%4))
        return out

def meet(peers):
    bar=pltpu.get_barrier_semaphore()
    for dev in peers:
        pl.semaphore_signal(bar,inc=1,device_id=dev,device_id_type=MESH)
    pl.semaphore_wait(bar,len(peers))

class Net:
    def __init__(self,send,recv):
        self.send,self.recv,self.k=send,recv,0
    def to(self,src,dst,dev):
        k=self.k; self.k+=1
        return pltpu.make_async_remote_copy(src_ref=src,dst_ref=dst,send_sem=self.send.at[k],recv_sem=self.recv.at[k],device_id=dev,device_id_type=MESH)

class Swap:
    def __init__(self,net,src,dst,dev,fixed):
        self.r=net.to(src,dst,dev); self.fixed=fixed
        self.l=pltpu.make_async_copy(src,dst,net.recv.at[net.k-1])
    def start(self):
        pl.when(jnp.logical_not(self.fixed))(self.r.start)
        pl.when(self.fixed)(self.l.start)
    def wait_recv(self): self.l.wait()
    def wait_send(self): pl.when(jnp.logical_not(self.fixed))(self.r.wait_send)

def rows(ref,start,size): return ref.at[pl.ds(start,size)]

NC=2
def gather_kernel(tok,ids,cot,wt,ck,ow,up,dn,upb,g1,s1,
                  x_all,ids_all,tok_p,cot_p,wt_p,ck_p,ow_a,up_a,dn_a,upb_a,
                  tokv,xn,send,recv,lsem):
    P=Place()
    meet(P.column()+[P.x,P.y,P.xy])
    net=Net(send,recv)
    n=tok.shape[0]; D=tok.shape[1]
    R=n//NC; H=R//2
    def swap(src,dst): return Swap(net,src,dst,P.dest,P.fixed)
    tk=[swap(rows(tok,k*R,R),rows(tokv,k*R,R)) for k in range(NC)]
    for c in tk: c.start()
    Q=wt.shape[0]//4
    w0=pl.multiple_of(P.quarter*Q,16)
    wq=swap(rows(wt,w0,Q),rows(wt_p,w0,Q)); wq.start()
    ckc=swap(ck,ck_p); ckc.start()
    idc=swap(ids,ids_all.at[4]); idc.start()
    def part(ref,tt):
        L=ref.shape[2]//2; r=ref.shape[1]//4
        return ref.at[tt,pl.ds(pl.multiple_of(P.quarter*r,16),r),pl.ds(pl.multiple_of(P.b*L,128),L)]
    def part_in(ref):
        L=ref.shape[1]//2; r=ref.shape[0]//4
        return ref.at[pl.ds(pl.multiple_of(P.quarter*r,16),r),pl.ds(pl.multiple_of(P.b*L,128),L)]
    ins=(ow,up,dn); alls=(ow_a,up_a,dn_a)
    own=[pltpu.make_async_copy(part_in(a),part(b,P.t),lsem.at[j]) for j,(a,b) in enumerate(zip(ins,alls))]
    for c in own: c.start()
    bias=[net.to(upb,upb_a.at[P.t],P.zed(r)) for r in (1,2,3)]
    for c in bias: c.start()
    ownb=pltpu.make_async_copy(upb,upb_a.at[P.t],lsem.at[3]); ownb.start()
    m=P.member
    halves={}
    for k in range(NC):
        tk[k].wait_recv()
        unit,_=ln(tokv[k*R:(k+1)*R,:].astype(F32))
        xn[k*R:(k+1)*R,:]=(unit*g1[...]+s1[...]).astype(BF)
        oh=pl.multiple_of(k*R+P.b*H,16); xh=pl.multiple_of(k*R+(1-P.b)*H,16)
        cs=[net.to(rows(xn,oh,H),x_all.at[m,pl.ds(oh,H)],P.opp),
            net.to(rows(xn,xh,H),x_all.at[m,pl.ds(xh,H)],P.cross),
            net.to(rows(xn,k*R,R),x_all.at[m,pl.ds(k*R,R)],P.sib)]
        for c in cs: c.start()
        halves[k]=cs
    ownx=pltpu.make_async_copy(xn,x_all.at[m],lsem.at[4]); ownx.start()
    ownt=pltpu.make_async_copy(tokv,tok_p,lsem.at[5]); ownt.start()
    cc=swap(cot,cot_p); cc.start()
    zs={}
    for r in (1,2,3):
        zs[r]=[net.to(part_in(a),part(b,P.t),P.zed(4-r)) for a,b in zip(ins,alls)]
        for c in zs[r]: c.start()
    idc.wait_recv()
    idown=pltpu.make_async_copy(ids_all.at[4],ids_all.at[m],lsem.at[6]); idown.start()
    idg=[net.to(ids_all.at[4],ids_all.at[m],dev) for dev in (P.sib,P.opp,P.cross)]
    for c in idg: c.start()
    wq.wait_recv()
    wf=[net.to(rows(wt_p,w0,Q),rows(wt_p,w0,Q),dev) for dev in (P.x,P.y,P.xy)]
    for c in wf: c.start()
    fw=[]
    om=2*(1-P.q)+P.b; xm=2*(1-P.q)+1-P.b
    for k in range(NC):
        oh=pl.multiple_of(k*R+P.b*H,16)
        for src,mm in ((0,om),(1,xm)):
            halves[k][src].wait_recv()
        a=net.to(x_all.at[om,pl.ds(oh,H)],x_all.at[om,pl.ds(oh,H)],P.sib)
        b=net.to(x_all.at[xm,pl.ds(oh,H)],x_all.at[xm,pl.ds(oh,H)],P.sib)
        a.start(); b.start(); fw+=[a,b]
    tail=[]
    for c in own: c.wait()
    for r in range(4):
        tt=(P.t+r)%4
        if r:
            for c in zs[r]: c.wait_recv()
        blk=[part(a,tt) for a in alls]
        one={}
        for name,dev in (("x",P.x),("y",P.y),("s",P.sib)):
            one[name]=[net.to(z,z,dev) for z in blk]
            for c in one[name]: c.start()
        def theirs(dq):
            out=[]
            for a in alls:
                L=a.shape[2]//2; rr=a.shape[1]//4
                out.append(a.at[tt,pl.ds(pl.multiple_of(dq*rr,16),rr),pl.ds(pl.multiple_of(P.b*L,128),L)])
            return out
        qx=(P.x[0]//2)%4; qy=(P.y[0]//2)%4; qd=(P.xy[0]//2)%4
        bx=theirs(qx); by=theirs(qy); bd=theirs(qd)
        for c in one["x"]: c.wait_recv()
        dg=[net.to(bx[0],bx[0],P.y),net.to(bx[1],bx[1],P.y)]
        for c in dg: c.start()
        sx=[net.to(z,z,P.sib) for z in bx]
        for c in sx: c.start()
        for c in one["y"]: c.wait_recv()
        dh=[net.to(by[2],by[2],P.x)]
        for c in dh: c.start()
        sy=[net.to(z,z,P.sib) for z in by]
        for c in sy: c.start()
        for c in dg+dh: c.wait_recv()
        sd=[net.to(z,z,P.sib) for z in bd]
        for c in sd: c.start()
        tail.append((one,dg+dh,sx+sy+sd))
    for r in range(4):
        one,dd,ss=tail[r]
        for c in one["s"]+ss: c.wait_recv()
        for c in one["x"]+one["y"]+one["s"]+dd+ss: c.wait_send()
        if r:
            for c in zs[r]: c.wait_send()
    for c in bias: c.wait()
    for c in idg: c.wait()
    for c in wf: c.wait()
    for k in range(NC):
        halves[k][2].wait_recv()
        for c in halves[k]: c.wait_send()
    for c in fw: c.wait()
    for c in tk+[wq,ckc,idc,cc]: c.wait_send()
    ckc.wait_recv(); cc.wait_recv()
    for c in (ownb,ownx,ownt,idown): c.wait()

def gather(tok,ids,cot,wt,ck,ow,up,dn,upb,g1,s1):
    n,D=tok.shape; S=jax.ShapeDtypeStruct
    any_=pl.BlockSpec(memory_space=pl.ANY); vm=pl.BlockSpec(memory_space=pltpu.VMEM)
    outs=(S((4,n,D),BF),S((5,1,n),jnp.int32),S((n,D),BF),S((n,D),BF),S(wt.shape,BF),S(ck.shape,F32),
          S((4,)+ow.shape,BF),S((4,)+up.shape,BF),S((4,)+dn.shape,BF),S((4,)+upb.shape,F32))
    return pl.pallas_call(gather_kernel,out_shape=outs,
        in_specs=[any_]*9+[vm]*2,out_specs=(any_,)*len(outs),
        scratch_shapes=[pltpu.VMEM((n,D),BF),pltpu.VMEM((n,D),BF),pltpu.SemaphoreType.DMA((140,)),pltpu.SemaphoreType.DMA((140,)),pltpu.SemaphoreType.DMA((8,))],
        compiler_params=pltpu.CompilerParams(collective_id=0,has_side_effects=True,vmem_limit_bytes=32*2**20),
        name="gather_inputs",
    )(tok,ids,cot,wt,ck,ow,up,dn,upb,g1,s1)

def lanes(start,size): return pl.ds(pl.multiple_of(start,128),size)
def rws(start,size): return pl.ds(pl.multiple_of(start,16),size)

def exchange_kernel(src,dst,send,recv,lsem):
    P=Place(); meet([P.sib,P.opp,P.cross])
    net=Net(send,recv); m=P.member
    ms=[2*P.q+1-P.b,2*(1-P.q)+P.b,2*(1-P.q)+1-P.b]
    cs=[net.to(src.at[k],dst.at[m],dev) for k,dev in zip(ms,(P.sib,P.opp,P.cross))]
    for c in cs[1:]+cs[:1]: c.start()
    own=pltpu.make_async_copy(src.at[m],dst.at[m],lsem.at[0]); own.start()
    for c in cs: c.wait()
    own.wait()

def exchange(x,cid,name):
    any_=pl.BlockSpec(memory_space=pl.ANY)
    return pl.pallas_call(exchange_kernel,out_shape=jax.ShapeDtypeStruct(x.shape,x.dtype),in_specs=[any_],out_specs=any_,
        scratch_shapes=[pltpu.SemaphoreType.DMA((4,)),pltpu.SemaphoreType.DMA((4,)),pltpu.SemaphoreType.DMA((1,))],
        compiler_params=pltpu.CompilerParams(collective_id=cid,has_side_effects=True),name=name)(x)

def reduce_kernel(gf,gm,tok,res,gow,gup,gdn,gw,small,g1,
                  res_o,gt_o,ow_o,up_o,dn_o,w_o,small_o,
                  land1,land2,land3,acc,gtv,
                  c_ow,c_up,c_dn,x_ow,x_up,y_dn,z_ow,z_up,z_dn,w1,w2,w3,f_ow,f_up,f_dn,f_w,sl,send,recv,lsem):
    P=Place(); meet(P.column()+[P.x,P.y,P.xy])
    net=Net(send,recv); m=P.member; b=P.b
    n=gm.shape[0]; D=gm.shape[1]; H=n//2; L=D//2
    f=lambda v: v.astype(F32)
    started=[]
    def push(src,dst,dev):
        c=net.to(src,dst,dev); c.start(); started.append(c); return c
    rs=Swap(net,res,res_o,P.source,P.fixed); rs.start()
    h0=pl.multiple_of(b*H,16); h1=pl.multiple_of((1-b)*H,16)
    e1=push(gf.at[:,pl.ds(h1,H),:],land1,P.sib)
    lo=P.b*L; lx=(1-P.b)*L
    cs=[push(a.at[:,:,lanes(lx,L)],z,P.sib) for a,z in ((gow,c_ow),(gup,c_up),(gdn,c_dn))]
    qr=P.quarter; qx=(P.x[0]//2)%4; qy=(P.y[0]//2)%4; qd=(P.xy[0]//2)%4
    def side(ref,k,rows_): return ref.at[:,rws(k*rows_,rows_),:]
    Q=gw.shape[0]//4
    wx=[push(gw.at[rws(k*Q,Q)],w1.at[j],P.x) for j,k in ((0,qx),(1,qd))]
    e1.wait_recv()
    for s in range(4):
        land1[s]=(f(land1[s])+f(gf[s,pl.ds(h0,H),:])).astype(BF)
    om=2*(1-P.q)
    e2=push(land1.at[pl.ds(om,2)],land2,P.opp)
    for c,a,z in zip(cs,(gow,gup,gdn),(c_ow,c_up,c_dn)):
        c.wait_recv()
        def add(t,_,a=a,z=z):
            z[t]=(f(z[t])+f(a[t,:,lanes(lo,L)])).astype(BF); return 0
        lax.fori_loop(0,4,add,0)
    ro,ru=gow.shape[1]//4,gup.shape[1]//4
    p1=[push(side(c_ow,k,ro),x_ow.at[j],P.x) for j,k in ((0,qx),(1,qd))]
    p1+=[push(side(c_up,k,ru),x_up.at[j],P.x) for j,k in ((0,qx),(1,qd))]
    p2=[push(side(c_dn,k,ru),y_dn.at[j],P.y) for j,k in ((0,qy),(1,qd))]
    e2.wait_recv()
    land2[0]=(f(land2[0])+f(land1[2*P.q])).astype(BF)
    land2[1]=(f(land2[1])+f(land1[2*P.q+1])).astype(BF)
    e3=push(land2.at[1-b],land3,P.sib)
    for c in wx: c.wait_recv()
    for j,k in ((0,qr),(1,qy)):
        w1[j]=(f(w1[j])+f(gw[rws(k*Q,Q)])).astype(BF)
    wy=push(w1.at[1],w2,P.y)
    e3.wait_recv()
    gtv[pl.ds(h0,H),:]=f(land2[b]); gtv[pl.ds(h1,H),:]=f(land3[...])
    unit,inv=ln(f(tok[...]))
    g=gtv[...]
    sl[5]=small[...]
    sl[5,4:5]=jnp.sum(g*unit,0,keepdims=True)
    sl[5,5:6]=jnp.sum(g,0,keepdims=True)
    acc[...]=(gm[...]+ln_back(g,unit,inv,g1[...])).astype(BF)
    gs=Swap(net,acc,gt_o,P.source,P.fixed); gs.start()
    sp=push(sl.at[5],sl.at[0],P.sib)
    for c in p1: c.wait_recv()
    for z,c0,r_ in ((x_ow,c_ow,ro),(x_up,c_up,ru)):
        for j,k in ((0,qr),(1,qy)):
            z[j]=(f(z[j])+f(c0[:,rws(k*r_,r_),:])).astype(BF)
    p3=[push(x_ow.at[1],z_ow.at[0],P.y),push(x_up.at[1],z_up.at[0],P.y)]
    for c in p2: c.wait_recv()
    for j,k in ((0,qr),(1,qx)):
        y_dn[j]=(f(y_dn[j])+f(c_dn[:,rws(k*ru,ru),:])).astype(BF)
    p4=push(y_dn.at[1],z_dn.at[0],P.x)
    sp.wait_recv(); sl[0]=sl[0]+sl[5]
    sp=push(sl.at[0],sl.at[1],P.x)
    wy.wait_recv()
    w1[0]=(f(w1[0])+f(w2[...])).astype(BF)
    wz=push(w1.at[0,:,lanes((1-P.p)*L,L)],w3.at[0],P.other)
    sp.wait_recv(); sl[1]=sl[1]+sl[0]
    sp=push(sl.at[1],sl.at[2],P.y)
    for c in p3+[p4]: c.wait_recv()
    zz=[]
    for z,own in ((z_ow,x_ow),(z_up,x_up),(z_dn,y_dn)):
        z[0]=(f(z[0])+f(own[0])).astype(BF)
        zz.append([push(z.at[0,1-P.q],z.at[1,0],P.opp),push(z.at[0,3-P.q],z.at[1,1],P.opp)])
    wz.wait_recv()
    w3[0]=(f(w3[0])+f(w1[0,:,lanes(P.p*L,L)])).astype(BF)
    ws=Swap(net,w3.at[0],w3.at[1],P.source,P.fixed); ws.start()
    sp.wait_recv(); sl[2]=sl[2]+sl[1]
    sp=push(sl.at[2],sl.at[3],P.opp)
    z2=[]
    for (z,fin),cc in zip(((z_ow,f_ow),(z_up,f_up),(z_dn,f_dn)),zz):
        for c in cc: c.wait_recv()
        for k in range(2):
            z[1,k]=(f(z[1,k])+f(z[0,2*k+P.q])).astype(BF)
        z2.append(push(z.at[1,1-P.p],fin.at[0],P.other))
    sp.wait_recv(); sl[3]=sl[3]+sl[2]
    sp=push(sl.at[3],sl.at[4],P.other)
    outs=((ow_o,f_ow,ro),(up_o,f_up,ru),(dn_o,f_dn,ru))
    def place(o,k,r_): return o.at[rws(k*r_,r_),lanes(lo,L)]
    ag=[]
    for (z,(o,fin,r_)),c in zip(zip((z_ow,z_up,z_dn),outs),z2):
        c.wait_recv()
        fin[1]=(f(fin[0])+f(z[1,P.p])).astype(BF)
        ag.append((o,fin.at[1],r_))
    ws.wait_recv()
    ag.append((w_o,w3.at[1],Q))
    ag=ag[::-1]
    own=[]; sx=[];sy=[];ss=[]
    for j,(o,s_,r_) in enumerate(ag):
        c=pltpu.make_async_copy(s_,place(o,qr,r_),lsem.at[j]); c.start(); own.append(c)
        sx.append(push(s_,place(o,qr,r_),P.x)); sy.append(push(s_,place(o,qr,r_),P.y)); ss.append(push(s_,place(o,qr,r_),P.sib))
    dg=[]
    for j,(o,s_,r_) in enumerate(ag):
        sx[j].wait_recv()
        if j%2==0: dg.append(push(place(o,qx,r_),place(o,qx,r_),P.y))
        ss.append(push(place(o,qx,r_),place(o,qx,r_),P.sib))
        sy[j].wait_recv()
        if j%2==1: dg.append(push(place(o,qy,r_),place(o,qy,r_),P.x))
        ss.append(push(place(o,qy,r_),place(o,qy,r_),P.sib))
    sp.wait_recv()
    small_o[...]=sl[4]+sl[3]
    for j,(o,s_,r_) in enumerate(ag):
        dg[j].wait_recv()
        ss.append(push(place(o,qd,r_),place(o,qd,r_),P.sib))
    for c in ss: c.wait_recv()
    for c in own: c.wait()
    for c in started: c.wait_send()
    for c in (rs,gs,ws): c.wait_send()
    rs.wait_recv(); gs.wait_recv()

def reduce(gf,gm,tok,res,gow,gup,gdn,gw,small,g1):
    S=jax.ShapeDtypeStruct; V=pltpu.VMEM
    any_=pl.BlockSpec(memory_space=pl.ANY); vm=pl.BlockSpec(memory_space=pltpu.VMEM)
    n,D=gm.shape; H=n//2; L=D//2
    a,bq=gow.shape[1],gup.shape[1]; w=gw.shape[0]; k=small.shape[0]
    outs=(S((n,D),BF),S((n,D),BF),S((a,D),BF),S((bq,D),BF),S((bq,D),BF),S((w,D),BF),S((k,D),F32))
    sc=[V((4,H,D),BF),V((2,H,D),BF),V((H,D),BF),V((n,D),BF),V((n,D),F32),
        V((4,a,L),BF),V((4,bq,L),BF),V((4,bq,L),BF),
        V((2,4,a//4,L),BF),V((2,4,bq//4,L),BF),V((2,4,bq//4,L),BF),
        V((2,4,a//4,L),BF),V((2,4,bq//4,L),BF),V((2,4,bq//4,L),BF),
        V((2,w//4,D),BF),V((w//4,D),BF),V((2,w//4,L),BF),
        V((2,a//4,L),BF),V((2,bq//4,L),BF),V((2,bq//4,L),BF),V((w//4,L),BF),V((6,k,D),F32),
        pltpu.SemaphoreType.DMA((80,)),pltpu.SemaphoreType.DMA((80,)),pltpu.SemaphoreType.DMA((8,))]
    return pl.pallas_call(reduce_kernel,out_shape=outs,
        in_specs=[vm,vm,vm,any_]+[vm]*6,out_specs=(any_,)*6+(vm,),scratch_shapes=sc,
        compiler_params=pltpu.CompilerParams(collective_id=3,has_side_effects=True,vmem_limit_bytes=60*2**20),name="reduce_gradients",
    )(gf,gm,tok,res,gow,gup,gdn,gw,small,g1)


def per_device(planes, tokens, segment_ids, cotangent, norm1_gain, norm1_shift, qkv_weight, conv_kernel, out_weight, out_bias, norm2_gain, norm2_shift, up_weight, up_bias, down_weight, down_bias):
    n, D = tokens.shape
    lw = qkv_weight.shape[2]
    row = lambda v: v.reshape(1, -1)
    wt = jnp.transpose(qkv_weight, (1, 2, 0)).reshape(3 * lw, D)
    x_all, ids_all, tok, cot, wtp, ckp, ow, up, dn, upb = gather(
        tokens, row(segment_ids), cotangent, wt, conv_kernel, out_weight, up_weight, down_weight, row(up_bias), row(norm1_gain), row(norm1_shift))
    x = x_all.reshape(4 * n, D)
    ids = ids_all[:4].reshape(1, 4 * n)
    ck = jnp.transpose(ckp, (1, 2, 0)).reshape(3 * lw, 3)
    att, proj, lse, of = attn_fwd(x, wtp, ck, ids, bq=512)
    att = exchange(att, 1, "exchange_attended").reshape(4 * lw, n)
    res, gm, ga, gow, gup, gdn, s4, gupb = ffn(
        att, tok, cot, ow.reshape(4 * lw, D), up, dn, row(out_bias), row(norm2_gain), row(norm2_shift), upb.reshape(4, -1), row(down_bias))
    ga = exchange(ga, 2, "exchange_grads")
    gf, gw, gc = attn_bwd(x, wtp, ck, ids, proj, lse, of, ga, B=512)
    d, t = lax.axis_index("dp"), lax.axis_index("tensor")
    member = 2 * (t % 2) + d % 2
    conv = jnp.zeros((4, 3, D), F32)
    conv = lax.dynamic_update_slice(conv, jnp.pad(gc.T, ((0, 0), (0, D - 3 * lw)))[None], (member, 0, 0)).reshape(12, D)
    small = jnp.concatenate([s4[:6], gupb, conv, jnp.zeros((2, D), F32)], 0)
    res, gt, ow_o, up_o, dn_o, w_o, sm = reduce(gf.reshape(4, n, D), gm, tok, res, gow.reshape(4, lw, D), gup, gdn, gw, small, row(norm1_gain))
    f = lambda v: v.astype(F32)
    sums = (f(w_o), f(ow_o), f(up_o), f(dn_o), sm)
    if planes is not None:
        sums = lax.psum(sums, "dp", axis_index_groups=planes)
    w_o, ow_o, up_o, dn_o, sm = sums
    gqkv = jnp.transpose(w_o.reshape(3, lw, D), (2, 0, 1))
    gck = lax.dynamic_slice(sm, (10 + 3 * t, 0), (3, 3 * lw)).reshape(3, 3, lw)
    gub = lax.dynamic_slice(sm, (6 + t, 0), (1, D)).reshape(-1)
    return (res, f(gt), sm[4], sm[5], gqkv, gck, ow_o, sm[0], sm[1], sm[2], up_o, gub, dn_o, sm[3])


def solution(mesh):
    dp = mesh.shape["dp"]
    planes = None
    if dp > 8:
        planes = [[8 * k + j for k in range(dp // 8)] for j in range(8)]
    rows_, rep = P_(("dp", "tensor"), None), P_()
    third, cols, first = P_(None, None, "tensor"), P_(None, "tensor"), P_("tensor", None)
    return jax.shard_map(
        functools.partial(per_device, planes),
        mesh=mesh,
        in_specs=(rows_, P_(("dp", "tensor")), rows_, rep, rep, third, third, first, rep, rep, rep, cols, P_("tensor"), first, rep),
        out_specs=(rows_, rows_, rep, rep, third, third, first, rep, rep, rep, cols, P_("tensor"), first, rep),
        check_vma=False,
    )
```

time: 1050 us -> 385 us (0.37)
  waiting for transfers between devices: 590 us -> 0 us
  Pallas kernels: 0 us -> 339 us
  matrix products: 211 us -> 0 us
  other arithmetic: 108 us -> 8.53 us
  blocking collectives: 80.3 us -> 0 us
  between operations: 14.8 us -> 0.99 us
  loops' own time: 13.6 us -> 0 us
    pallas_call x0 -> x7, Pallas kernels: none -> 339 us  [the longest x1 115 us: reduce(): pl.pallas_call(reduce_kernel, out_shape=outs, in_specs=[vm, vm, vm, any_]...]
    reduce_scatter x4 -> x0, waiting for transfers between devices: 281 us -> none  [the longest x1 109 us: per_device(): lax.psum_scatter(jnp.dot(att_low, out_weight, preferred_element_type=jnp....]
    all_gather x4 -> x0, waiting for transfers between devices: 236 us -> none  [the longest x1 63.6 us: per_device(): lax.all_gather(grad_middle.astype(jnp.bfloat16), 'tensor', axis=0, tiled=...]
    dot_general x40 -> x0, matrix products: 211 us -> none  [the longest x8 35.9 us: block_scores(): jnp.einsum('qhd,khd->hqk', query_block, key_rows, preferred_element_type=...]
    psum x1 -> x0, waiting for transfers between devices: 72.7 us -> none  [per_device(): lax.psum((grad_qkv, grad_kernel, grad_outw, grad_up, grad_upb, grad_down)...]
    psum x2 -> x0, blocking collectives: 66.8 us -> none  [the longest x1 41.5 us: per_device(): lax.psum((grad_gain_one, grad_shift_one, grad_outb, grad_gain_two, grad_s...]
    reduce_sum x13 -> x0, other arithmetic: 53.7 us -> none  [the longest x4 27.3 us: one_block(): row_total = jnp.sum(exps, -1, keepdims=True)]
    convert_element_type x9 -> x4, other arithmetic: 34.1 us -> 6.47 us  [per_device(): f = lambda v: v.astype(F32)]
  transfers between devices with their start and end apart: 9 -> 0, of which waited for: 9 -> 0; matrix products, arithmetic and copies ran while one was open for 4% -> 0% of each run, Pallas kernels for 0% -> 0%
where the time goes in v1:
time: 385 us; the launch traced here: 378 us
  Pallas kernels  339 us (88%)
  local copies, waits for them, and re-layouts  30.1 us (8%)
  other arithmetic  8.53 us (2%)
    pallas_call x1, Pallas kernels, reduce(): pl.pallas_call(reduce_kernel, out_shape=outs, in_specs=[vm, vm, vm, any_]...  115 us
    pallas_call x1, Pallas kernels, gather(): pl.pallas_call(gather_kernel, out_shape=outs, in_specs=[any_] * 9 + [vm]...  102 us
    pallas_call x1, Pallas kernels, attn_bwd(): pl.pallas_call(functools.partial(bwd_kernel, n, heads, B), out_shape=(jax...  40.9 us
    pallas_call x2, Pallas kernels, exchange(): pl.pallas_call(exchange_kernel, out_shape=jax.ShapeDtypeStruct(x.shape, x...  32.5 us
    pallas_call x1, Pallas kernels, ffn(): pl.pallas_call(ffn_kernel, out_shape=(S((n, D), BF), S((n, D), F32), S((T...  28.8 us
    unnamed x56, local copies, waits for them, and re-layouts  19.7 us
    pallas_call x1, Pallas kernels, attn_fwd(): pl.pallas_call(functools.partial(fwd_kernel, n, heads, bq), out_shape=(ja...  19.6 us

profile of v1, /device:TPU:0, one launch (start us, length us, event | category | flops | bytes accessed | tf_op | source)
XLA Modules:
  0.0 378.5 jit_solution(11393648470447080682)
XLA Ops:
  0.6 0.7 reshape.95.upb
  1.3 0.7 reshape.96.g1
  2.0 0.0 copy-start.13
  2.0 0.7 reshape.97.s1
  2.7 0.0 copy-start.5
  2.7 1.3 copy-done.5
  4.0 0.0 copy-start.6
  4.0 1.3 copy-done.6
  5.3 1.2 copy-done.8
  6.4 1.1 copy-done.9
  7.6 1.1 copy-done.10
  8.7 1.0 copy-done.12
  9.7 0.7 copy-done.14
  10.4 0.7 copy-done.15
  11.0 101.6 %gather_inputs.1 = (bf16[4,512,768]{2,1,0:T(8,128)(2,1)S(1)}, s32[5,1,512]{2,1,0:T(1,128)S(1)}, bf16[512,768]{1,0:T(8,128)(2,1)S(1)}, bf16[512,768]{1,0:T(8,128)...) custom-call(bf16[512,768]{1,0:T(8,128)(2,1)S(1)} %copy-done.9, ...), custom_call_target="tpu_custom_call" | custom-call | tf_op jit(solution)/shard_map/gather_inputs/pallas_call | solution.py:413
  112.7 0.0 copy-done.13
  112.7 0.0 copy-start
  112.7 1.7 copy-done
  114.4 2.1 copy-done.1
  116.5 2.2 copy-done.2
  118.7 0.9 copy-done.3
  119.6 0.9 copy-done.4
  120.5 1.0 copy-done.7
  121.5 0.9 copy-done.11
  122.4 0.9 copy.31
  123.3 0.6 slice.24
  123.9 19.6 %shard_map.254 = (bf16[4,192,512]{2,1,0:T(8,128)(2,1)}, f32[576,2048]{1,0:T(8,128)}, f32[3,8,2048]{2,1,0:T(8,128)}, f32[192,2048]{1,0:T(8,128)}) custom-call(bf16[2048,768]{1,0:T(8,128)(2,1)} %bitcast.23, bf16[576,768]{1,0:T(8,128)(2,1)} %copy-done.3, f32[576,3]{1,0:T(8,128)} %bitcast.31, s32[1,2048]{1,0:T(1,128)} %bitcast.36), custom_call_target="tpu_custom_call" | custom-call | tf_op jit(solution)/shard_map/pallas_call | solution.py:88
  143.5 21.1 %exchange_attended.1 = bf16[4,192,512]{2,1,0:T(8,128)(2,1)} custom-call(bf16[4,192,512]{2,1,0:T(8,128)(2,1)} %get-tuple-element.53.src), custom_call_target="tpu_custom_call" | custom-call | tf_op jit(solution)/shard_map/exchange_attended/pallas_call | solution.py:435
  164.6 0.0 copy-done.23
  164.6 0.6 reshape.103.outb
  165.2 0.0 copy-done.24
  165.2 0.6 reshape.104.g2
  165.8 0.0 copy-done.25
  165.8 0.6 reshape.105.s2
  166.4 0.6 copy.35
  167.0 0.0 copy-done.26
  167.0 0.6 reshape.107.dnb
  167.6 28.8 %shard_map.255 = (bf16[512,768]{1,0:T(8,128)(2,1)}, f32[512,768]{1,0:T(8,128)}, bf16[4,192,512]{2,1,0:T(8,128)(2,1)}, bf16[768,768]{1,0:T(8,128)(2,1)}, bf16[4,7...) custom-call(bf16[768,512]{1,0:T(8,128)(2,1)} %bitcast.29, ...), custom_call_target="tpu_custom_call" | custom-call | tf_op jit(solution)/shard_map/pallas_call | solution.py:234
  196.3 11.5 %exchange_grads.1.ga_ref = bf16[4,192,512]{2,1,0:T(8,128)(2,1)} custom-call(bf16[4,192,512]{2,1,0:T(8,128)(2,1)} %get-tuple-element.60.src), custom_call_target="tpu_custom_call" | custom-call | tf_op jit(solution)/shard_map/exchange_grads/pallas_call | solution.py:435
  207.8 0.0 copy-start.21
  207.8 0.0 copy-start.22
  207.8 40.9 %shard_map.256 = (bf16[2048,768]{1,0:T(8,128)(2,1)}, bf16[576,768]{1,0:T(8,128)(2,1)}, f32[576,3]{1,0:T(8,128)}) custom-call(bf16[2048,768]{1,0:T(8,128)(2,1)} %bitcast.24, bf16[576,768]{1,0:T(8,128)(2,1)} %copy-done.3, f32[576,3]{1,0:T(8,128)} %bitcast.32, s32[1,2048]{1,0:T(1,128)} %bitcast.37, f32[576,2048]{1,0:T(8,128)} %get-tuple-element.50.proj_ref, ...), custom_call_target="tpu_custom_call" | custom-call | tf_op jit(solution)/shard_map/pallas_call | solution.py:174
  248.7 1.0 pad_bitcast_fusion
  249.7 0.1 copy.32
  250.0 0.1 pad.8.clone
  250.0 0.0 copy-done.21
  250.0 0.0 copy-done.22
  250.0 0.7 maximum_maximum_fusion.small
  250.8 115.4 %reduce_gradients.1 = (bf16[512,768]{1,0:T(8,128)(2,1)}, bf16[512,768]{1,0:T(8,128)(2,1)}, bf16[192,768]{1,0:T(8,128)(2,1)}, bf16[768,768]{1,0:T(8,128)(2,1)}, b...) custom-call(bf16[4,512,768]{2,1,0:T(8,128)(2,1)} %bitcast.30, ...), custom_call_target="tpu_custom_call" | custom-call | tf_op jit(solution)/shard_map/reduce_gradients/pallas_call | solution.py:571
  366.2 0.0 copy-start.18
  366.2 2.5 convert_element_type.15
  368.7 1.8 slice_reduce_fusion
  370.5 0.0 copy-done.18
  370.5 1.4 convert_bitcast_fusion
  371.8 0.8 constant_dynamic-slice_fusion
  372.6 0.7 reshape.112
  373.3 0.0 copy-done.20
  373.3 0.9 convert_element_type.16
  374.2 0.0 copy-done.17
  374.2 1.6 convert_element_type.17
  375.7 0.1 copy-done.16
  375.8 1.6 convert_element_type.18
  377.4 0.0 copy-done.19
  377.4 0.9 copy.38
  (24 shorter events, 0.1 us)
Async XLA Ops:
  2.0 110.7 %copy-start.13 = (f32[1,768]{1,0:T(1,128)}, f32[1,768]{1,0:T(1,128)S(1)}, u32[]{:S(2)}) copy-start(f32[1,768]{1,0:T(1,128)S(1)} %reshape.96.g1) | copy-start | bytes 9220
  2.7 1.3 copy-start.5
  4.0 1.3 copy-start.6
  5.3 1.2 copy-start.8
  6.4 1.1 copy-start.9
  7.6 1.1 copy-start.10
  8.7 1.0 copy-start.12
  9.7 0.7 copy-start.14
  10.4 0.7 copy-start.15
  112.7 1.7 copy-start
  114.4 2.1 copy-start.1
  116.5 2.2 copy-start.2
  118.7 0.9 copy-start.3
  119.6 0.9 copy-start.4
  120.5 1.0 copy-start.7
  121.5 0.9 copy-start.11
  123.9 40.7 %copy-start.23 = (f32[768]{0:T(1024)S(1)}, f32[768]{0:T(1024)}, u32[]{:S(2)}) copy-start(f32[768]{0:T(1024)} %param.23) | copy-start | bytes 9220
  123.9 41.3 %copy-start.24 = (f32[768]{0:T(1024)S(1)}, f32[768]{0:T(1024)}, u32[]{:S(2)}) copy-start(f32[768]{0:T(1024)} %param.24) | copy-start | bytes 9220
  123.9 41.9 %copy-start.25 = (f32[768]{0:T(1024)S(1)}, f32[768]{0:T(1024)}, u32[]{:S(2)}) copy-start(f32[768]{0:T(1024)} %param.25) | copy-start | bytes 9220
  123.9 43.1 %copy-start.26 = (f32[768]{0:T(1024)S(1)}, f32[768]{0:T(1024)}, u32[]{:S(2)}) copy-start(f32[768]{0:T(1024)} %param.29) | copy-start | bytes 9220
  207.8 42.3 %copy-start.21 = (f32[8,768]{1,0:T(8,128)S(1)}, f32[8,768]{1,0:T(8,128)}, u32[]{:S(2)}) copy-start(f32[8,768]{1,0:T(8,128)} %get-tuple-element.68) | copy-start | bytes 73732
  207.8 42.3 %copy-start.22 = (f32[4,768]{1,0:T(4,128)S(1)}, f32[4,768]{1,0:T(4,128)}, u32[]{:S(2)}) copy-start(f32[4,768]{1,0:T(4,128)} %get-tuple-element.69) | copy-start | bytes 36868
  366.2 4.3 %copy-start.18 = (bf16[576,768]{1,0:T(8,128)(2,1)S(1)}, bf16[576,768]{1,0:T(8,128)(2,1)}, u32[]{:S(2)}) copy-start(bf16[576,768]{1,0:T(8,128)(2,1)} %get-tuple-element.74) | copy-start | bytes 2654212
  368.7 4.6 %copy-start.20 = (bf16[192,768]{1,0:T(8,128)(2,1)S(1)}, bf16[192,768]{1,0:T(8,128)(2,1)}, u32[]{:S(2)}) copy-start(bf16[192,768]{1,0:T(8,128)(2,1)} %get-tuple-element.75) | copy-start | bytes 884740
  370.5 3.7 copy-start.17
  374.2 1.7 copy-start.16
  375.8 1.6 copy-start.19
